TPU v7x, 128 devices: a whole 4x4x4 slice. The times are simulated.
128 devices in a mesh: row: 8 (over y, z_lo), col: 16 (over z_hi, x, core).
Axes of the slice: x: 4, y: 4, z: 4 (z_hi: 2, z_lo: 2; z = z_hi * 2 + z_lo), core: 2. Of those that a mesh axis runs over, the one named last changes fastest.
Arguments:
- velocity: float32 [3, 4, 512, 2048], P(None, None, 'row', 'col'), may hold values from -6 to 6
- stress: float32 [6, 4, 512, 2048], P(None, None, 'row', 'col'), may hold values from -6 to 6
- buoyancy: float32 [4, 512, 2048], P(None, 'row', 'col'), may hold values from 0.2 to 0.4
- lame: float32 [4, 512, 2048], P(None, 'row', 'col'), may hold values from 0.08 to 0.2
- shear: float32 [4, 512, 2048], P(None, 'row', 'col'), may hold values from 0.08 to 0.2
- kernel: bfloat16 [12, 3, 2, 2048, 512], P(None, None, None, ('row', 'col')), may hold values from -1.1953125 to 1.1953125
- history: bfloat16 [11, 3, 2, 2048, 512], P(None, None, None, ('row', 'col')), may hold values from -6 to 6
Outputs:
- new_velocity: float32 [3, 4, 512, 2048], P(None, None, 'row', 'col')
- new_stress: float32 [6, 4, 512, 2048], P(None, None, 'row', 'col')
- spectra: float32 [2, 3, 2, 2048, 512], P(None, None, None, ('row', 'col'))
All inputs are finite; a program needn't handle non-finite values.
Results may differ from a plain program's by a relative error of at most 0.0003.
Values sent between devices are 32-bit elements; how exact they have to be, the bound alone decides.
A program may use at most 128 MiB of HBM per device.

v0:
```python
import math

import jax
import jax.numpy as jnp
import numpy as np
from jax import lax
from jax.experimental import pallas as pl
from jax.experimental.pallas import tpu as pltpu
from jax.sharding import PartitionSpec as P

MESH = pl.DeviceIdType.MESH
F32, BF16 = jnp.float32, jnp.bfloat16
ROWS, COLS, DEVS = 8, 16, 128
NEAR, FAR = 2.0 / 3.0, -1.0 / 12.0
PLACE = (0, 3, 4, 1, 5, 2)
XX, XY, XZ, YY, YZ, ZZ = range(6)


def tables():
    def halves(a):
        hi = a.astype(BF16)
        lo = (a - hi.astype(np.float64)).astype(BF16)
        return hi, lo

    i128 = np.arange(128)
    ang = 2 * np.pi * (np.outer(i128, i128) % 128) / 128
    cos, sin = np.cos(ang), np.sin(ang)
    hi, lo = halves(np.concatenate([cos, sin], axis=1))
    left = np.concatenate([hi, hi, lo], axis=1)
    right = np.concatenate([hi, hi, lo], axis=0)
    j, c = np.arange(16), np.arange(16)
    ang = 2 * np.pi * (np.outer(j, c) % 16) / 16
    one = np.zeros((2, 4, 16, 16, 4))
    for xl in range(4):
        one[0, xl, :, :, xl] = np.cos(ang)
        one[1, xl, :, :, xl] = -np.sin(ang)
    one = one.reshape(128, 64) / 1024.0
    hi, lo = halves(one)
    first = np.concatenate([hi, hi, lo, lo], axis=1)
    hi, lo = halves(one.T)
    last = np.concatenate([hi, hi, lo], axis=1)
    small = np.zeros((48, 128), np.float32)
    ang = 2 * np.pi * np.outer(j, i128) / 2048
    small[0:16], small[16:32] = np.cos(ang), np.sin(ang)
    ang = 2 * np.pi * np.outer(np.arange(4), i128) / 512
    small[32:36], small[36:40] = np.cos(ang), np.sin(ang)
    th = 2 * np.pi * np.arange(512) / 512
    small[40:44] = (4 / 3 * np.sin(th) - 1 / 6 * np.sin(2 * th)).reshape(4, 128)
    th = 2 * np.pi * np.arange(2048) / 2048
    along = (4 / 3 * np.sin(th) - 1 / 6 * np.sin(2 * th)).reshape(128, 16, 1)
    along = np.broadcast_to(along, (128, 16, 128)).astype(np.float32)
    return left, right, first, last, small, along


def halves(x):
    hi = x.astype(BF16)
    return hi, (x - hi.astype(F32)).astype(BF16)


def dot(a, b, contract=((1,), (0,))):
    return lax.dot_general(a, b, (contract, ((), ())), preferred_element_type=F32)


def kernel_body(
    vel_in, str_in, buo_in, lam_in, she_in, ker_in, his_in,
    left_in, right_in, first_in, last_in, small_in, along_in,
    vel_out, str_out, spe_out,
    vpad, spad, coef, ker, his, left, right, first, last, small, along,
    pack, pack_low, pack_high, rows_in, buo_rows, send_a, recv_a, send_b, recv_b,
    rows_out, trac, part, spec,
    in_sem, out_sem, halo_send, halo_recv, col_send, col_recv, all_send, all_recv, own_sem,
):
    r, c = lax.axis_index("row"), lax.axis_index("col")
    me = r * COLS + c

    loads = []

    def load(src, dst):
        copy = pltpu.make_async_copy(src, dst, in_sem.at[len(loads)])
        copy.start()
        loads.append(copy)
        return copy

    stress_loads = [
        load(str_in.at[PLACE[k]], spad.at[k, :, pl.ds(8, 64), :]) for k in range(6)
    ]
    coef_loads = [load(buo_in, coef.at[0])]
    vel_load = load(vel_in, vpad.at[:, :, pl.ds(8, 64), :])
    conv_loads = [load(ker_in, ker), load(his_in, his)]
    table_loads = [
        load(left_in, left), load(right_in, right), load(first_in, first),
        load(last_in, last), load(small_in, small), load(along_in.at[me], along),
    ]
    coef_late = [load(lam_in, coef.at[1]), load(she_in, coef.at[2])]

    def device(k):
        t = lax.rem(me + k, DEVS)
        return (t // COLS, lax.rem(t, COLS))

    barrier = pltpu.get_barrier_semaphore()

    def greet(k, _):
        pl.semaphore_signal(barrier, inc=1, device_id=device(k), device_id_type=MESH)
        return 0

    lax.fori_loop(1, DEVS, greet, 0)

    up, down = (lax.rem(r + 1, ROWS), c), (lax.rem(r + ROWS - 1, ROWS), c)
    after, before = (r, lax.rem(c + 1, COLS)), (r, lax.rem(c + COLS - 1, COLS))

    lane = lax.broadcasted_iota(jnp.int32, (64, 128), 1)
    edge = jnp.logical_or(lane < 2, lane >= 126)

    def start_halo(n, pad, count, arrays):
        packed = jnp.zeros((64, 128), F32)
        for k, (comp, layer) in enumerate(arrays):
            f = pad[comp, layer, pl.ds(8, 64), :]
            packed += pltpu.roll(jnp.where(edge, f, 0.0), 4 * k + 2, 1)
        pack[n] = packed

        def remote(i, src, dst, to):
            copy = pltpu.make_async_remote_copy(
                src_ref=src, dst_ref=dst, send_sem=halo_send.at[n, i],
                recv_sem=halo_recv.at[n, i], device_id=to, device_id_type=MESH,
            )
            return copy

        copies = [
            remote(0, pad.at[pl.ds(0, count), :, pl.ds(64, 8), :],
                   pad.at[pl.ds(0, count), :, pl.ds(0, 8), :], up),
            remote(1, pad.at[pl.ds(0, count), :, pl.ds(8, 8), :],
                   pad.at[pl.ds(0, count), :, pl.ds(72, 8), :], down),
            remote(2, pack.at[n], pack_low.at[n], after),
            remote(3, pack.at[n], pack_high.at[n], before),
        ]
        return copies

    def edges_of(n):
        return jnp.where(lax.rem(lane, 4) >= 2, pack_high[n], pack_low[n])

    def dx(pad, comp, layer):
        def at(o):
            return pad[comp, layer, pl.ds(8 + o, 64), :]

        return NEAR * (at(1) - at(-1)) + FAR * (at(2) - at(-2))

    def dy(f, both, k):
        e = pltpu.roll(both, 128 - (4 * k + 2), 1)
        p1 = pltpu.roll(jnp.where(lane == 0, e, f), 127, 1)
        p2 = pltpu.roll(jnp.where(lane < 2, e, f), 126, 1)
        m1 = pltpu.roll(jnp.where(lane == 127, e, f), 1, 1)
        m2 = pltpu.roll(jnp.where(lane >= 126, e, f), 2, 1)
        return NEAR * (p1 - m1) + FAR * (p2 - m2)

    def dz(pad, comp, layer):
        total = None
        for o, w in ((1, NEAR), (-1, -NEAR), (2, FAR), (-2, -FAR)):
            if 0 <= layer + o < 4:
                term = w * pad[comp, layer + o, pl.ds(8, 64), :]
                total = term if total is None else total + term
        return total

    stress_y = [(k, l) for k in (XY, YY, YZ) for l in range(4)]
    vel_y = [(k, l) for k in range(3) for l in range(4)]

    def new_velocity(both, layer):
        along_x = [dx(spad, k, layer) for k in (XX, XY, XZ)]
        along_y = [
            dy(spad[k, layer, pl.ds(8, 64), :], both, 4 * i + layer)
            for i, k in enumerate((XY, YY, YZ))
        ]
        along_z = [dz(spad, k, layer) for k in (XZ, YZ, ZZ)]
        b = coef[0, layer]
        for i in range(3):
            vpad[i, layer, pl.ds(8, 64), :] = vpad[i, layer, pl.ds(8, 64), :] + b * (
                along_x[i] + along_y[i] + along_z[i]
            )

    def new_stress(both, layer):
        gx = [dx(vpad, i, layer) for i in range(3)]
        gy = [dy(vpad[i, layer, pl.ds(8, 64), :], both, 4 * i + layer) for i in range(3)]
        gz = [dz(vpad, i, layer) for i in range(3)]
        lam, she = coef[1, layer], coef[2, layer]
        spread = lam * (gx[0] + gy[1] + gz[2])
        adds = {
            XX: spread + 2.0 * she * gx[0], YY: spread + 2.0 * she * gy[1],
            ZZ: spread + 2.0 * she * gz[2], XY: she * (gy[0] + gx[1]),
            XZ: she * (gz[0] + gx[2]), YZ: she * (gz[1] + gy[2]),
        }
        for k, a in adds.items():
            spad[k, layer, pl.ds(8, 64), :] = spad[k, layer, pl.ds(8, 64), :] + a

    def send_rows(n, src, dst):
        def one(k, _):
            t = lax.rem(c + k, COLS)
            pltpu.make_async_remote_copy(
                src_ref=src(t), dst_ref=dst(c), send_sem=col_send.at[n],
                recv_sem=col_recv.at[n], device_id=(r, t), device_id_type=MESH,
            ).start()
            return 0

        lax.fori_loop(1, COLS, one, 0)
        own = pltpu.make_async_copy(src(c), dst(c), own_sem.at[n])
        own.start()
        return own

    def wait_rows(n, own, whole):
        copy = pltpu.make_async_remote_copy(
            src_ref=whole, dst_ref=whole, send_sem=col_send.at[n],
            recv_sem=col_recv.at[n], device_id=after, device_id_type=MESH,
        )
        copy.wait()
        own.wait()

    def four(t):
        return pl.ds(pl.multiple_of(4 * t, 4), 4)

    def send_top(n):
        return send_rows(
            n, lambda t: vpad.at[:, 0, pl.ds(pl.multiple_of(8 + 4 * t, 4), 4), :],
            lambda t: rows_in.at[n // 2, :, four(t), :],
        )

    def wait_top(n, own):
        wait_rows(n, own, rows_in.at[n // 2, :, pl.ds(0, 60), :])

    def send_traction(n, count):
        return send_rows(
            n, lambda t: rows_out.at[n // 2, pl.ds(0, count), four(t), :],
            lambda t: trac.at[n // 2, pl.ds(0, count), four(t), :],
        )

    def wait_traction(n, own, count):
        wait_rows(n, own, trac.at[n // 2, pl.ds(0, count), pl.ds(0, 60), :])

    def send_all(n, src, dst):
        def one(k, _):
            t = lax.rem(me + k, DEVS)
            pltpu.make_async_remote_copy(
                src_ref=src.at[t], dst_ref=dst.at[me], send_sem=all_send.at[n],
                recv_sem=all_recv.at[n], device_id=device(k), device_id_type=MESH,
            ).start()
            return 0

        lax.fori_loop(1, DEVS, one, 0)
        own = pltpu.make_async_copy(src.at[me], dst.at[me], own_sem.at[5 + n])
        own.start()
        return own

    def wait_all(n, own, dst):
        whole = dst.at[pl.ds(0, DEVS - 1)]
        copy = pltpu.make_async_remote_copy(
            src_ref=whole, dst_ref=whole, send_sem=all_send.at[n],
            recv_sem=all_recv.at[n], device_id=after, device_id_type=MESH,
        )
        copy.wait()
        own.wait()

    def turn(re, im, cos, sin, sign):
        return re * cos - im * (sign * sin), im * cos + re * (sign * sin)

    def to_send(blocks, sign, out):
        data = []
        for re, im in blocks:
            data.append(jnp.concatenate([re, -sign * im], axis=1))
            data.append(jnp.concatenate([im, sign * re], axis=1))
        hi, lo = halves(jnp.concatenate(data, axis=0))
        full = dot(left[...], jnp.concatenate([hi, lo, hi], axis=1), ((1,), (1,)))
        for i in range(len(blocks)):
            out[:, i, :] = full[:, 128 * i : 128 * i + 128]

    def from_recv(buf, which, sign):
        turned = [buf[:, i, :].T for i in which]
        hi, lo = halves(jnp.concatenate(turned, axis=0))
        full = dot(jnp.concatenate([hi, lo, hi], axis=1), right[...])
        result = []
        for i in range(len(turned)):
            a = full[128 * i : 128 * i + 128]
            p, q = a[:, :128], a[:, 128:]
            result.append((p[:64] - sign * q[64:], p[64:] + sign * q[:64]))
        return result

    def rows_forward(fields, out):
        hi, lo = halves(jnp.concatenate(fields, axis=1))
        mixed = dot(first[...], jnp.concatenate([hi, lo, hi, lo], axis=0))
        cos, sin = small[0:16][None], small[16:32][None]
        blocks = []
        for i in range(len(fields)):
            a = mixed[:, 128 * i : 128 * i + 128]
            re, im = a[:64].reshape(4, 16, 128), a[64:].reshape(4, 16, 128)
            re, im = turn(re, im, cos, sin, -1.0)
            blocks.append((re.reshape(64, 128), im.reshape(64, 128)))
        to_send(blocks, -1.0, out)

    def rows_inverse(buf, which):
        cos, sin = small[0:16][None], small[16:32][None]
        parts = []
        for re, im in from_recv(buf, which, 1.0):
            re, im = turn(re.reshape(4, 16, 128), im.reshape(4, 16, 128), cos, sin, 1.0)
            parts.append(
                jnp.concatenate([re.reshape(64, 128), im.reshape(64, 128)], axis=0)
            )
        hi, lo = halves(jnp.concatenate(parts, axis=1))
        full = dot(last[...], jnp.concatenate([hi, lo, hi], axis=0))
        return [full[:, 128 * i : 128 * i + 128] for i in range(len(parts))]

    def spectrum_forward(buf, step):
        for i, (re, im) in enumerate(from_recv(buf, (0, 1, 2), -1.0)):
            a = []
            for xl in range(4):
                cos, sin = small[32 + xl : 33 + xl], small[36 + xl : 37 + xl]
                b = re[16 * xl : 16 * xl + 16], im[16 * xl : 16 * xl + 16]
                a.append(b if xl == 0 else turn(*b, cos, sin, -1.0))
            for k, (zr, zi) in enumerate(quarter(a, -1.0)):
                spec[step, i, 0, :, 128 * k : 128 * k + 128] = zr
                spec[step, i, 1, :, 128 * k : 128 * k + 128] = zi

    def quarter(a, sign):
        (ar, ai), (br, bi), (cr, ci), (dr, di) = a
        pr, pi, mr, mi = ar + cr, ai + ci, ar - cr, ai - ci
        qr, qi, nr, ni = br + dr, bi + di, br - dr, bi - di
        tr, ti = -sign * ni, sign * nr
        return ((pr + qr, pi + qi), (mr + tr, mi + ti), (pr - qr, pi - qi), (mr - tr, mi - ti))

    def spectrum_inverse(loads_, out):
        blocks = []
        for re, im in loads_:
            a = [(re[:, 128 * k : 128 * k + 128], im[:, 128 * k : 128 * k + 128]) for k in range(4)]
            res, ims = [], []
            for xl, (zr, zi) in enumerate(quarter(a, 1.0)):
                if xl:
                    cos, sin = small[32 + xl : 33 + xl], small[36 + xl : 37 + xl]
                    zr, zi = turn(zr, zi, cos, sin, 1.0)
                res.append(zr)
                ims.append(zi)
            blocks.append((jnp.concatenate(res, axis=0), jnp.concatenate(ims, axis=0)))
        to_send(blocks, 1.0, out)

    def convolve_past(step):
        for i in range(3):
            def lag(m, acc):
                kr, ki = ker[m, i, 0].astype(F32), ker[m, i, 1].astype(F32)
                hr, hi = his[m - 1 - step, i, 0].astype(F32), his[m - 1 - step, i, 1].astype(F32)
                return acc[0] + (kr * hr - ki * hi), acc[1] + (kr * hi + ki * hr)

            zero = jnp.zeros((16, 512), F32)
            re, im = lax.fori_loop(1 + step, 12, lag, (zero, zero))
            part[step, i, 0], part[step, i, 1] = re, im

    def add_lag(i, m, step, re, im):
        kr, ki = ker[m, i, 0].astype(F32), ker[m, i, 1].astype(F32)
        sr, si = spec[step, i, 0], spec[step, i, 1]
        return re + (kr * sr - ki * si), im + (kr * si + ki * sr)

    for copy in stress_loads:
        copy.wait()
    halo = start_halo(0, spad, 3, stress_y)
    pl.semaphore_wait(barrier, DEVS - 1)
    for copy in halo:
        copy.start()
    for copy in coef_loads:
        copy.wait()
    own_b = send_rows(4, lambda t: coef.at[0, 0, four(t), :], lambda t: buo_rows.at[four(t), :])
    for copy in conv_loads:
        copy.wait()
    convolve_past(0)
    vel_load.wait()
    for copy in halo:
        copy.wait()
    both = edges_of(0)
    new_velocity(both, 0)
    own = send_top(0)
    for layer in range(1, 4):
        new_velocity(both, layer)
    halo = start_halo(1, vpad, 3, vel_y)
    for copy in halo:
        copy.start()
    for copy in table_loads:
        copy.wait()
    wait_top(0, own)
    rows_forward([rows_in[0, i] for i in range(3)], send_a.at[0])
    own = send_all(0, send_a.at[0], recv_a.at[0])

    for copy in coef_late:
        copy.wait()
    for copy in halo:
        copy.wait()
    both = edges_of(1)
    for layer in range(4):
        new_stress(both, layer)
    halo = start_halo(2, spad, 3, stress_y)
    for copy in halo:
        copy.start()

    wait_all(0, own, recv_a.at[0])
    spectrum_forward(recv_a.at[0], 0)
    now = [add_lag(i, 0, 0, part[0, i, 0], part[0, i, 1]) for i in range(3)]
    ax = [small[40 + k : 41 + k] for k in range(4)]
    ay = along[...]

    def slope(xs, ys):
        return jnp.concatenate(
            [
                ax[k] * xs[:, 128 * k : 128 * k + 128] + ay * ys[:, 128 * k : 128 * k + 128]
                for k in range(4)
            ],
            axis=1,
        )

    slopes = (-slope(now[0][1], now[1][1]), slope(now[0][0], now[1][0]))
    spectrum_inverse([*now, slopes], send_b.at[0])
    own = send_all(1, send_b.at[0], recv_b.at[0])

    for copy in halo:
        copy.wait()
    both = edges_of(2)
    new_velocity(both, 0)
    own_top = send_top(2)
    for layer in range(1, 4):
        new_velocity(both, layer)
    convolve_past(1)
    for i in range(3):
        re, im = add_lag(i, 1, 0, part[1, i, 0], part[1, i, 1])
        part[1, i, 0], part[1, i, 1] = re, im
    wait_rows(4, own_b, buo_rows.at[pl.ds(0, 60), :])
    wait_top(2, own_top)

    wait_all(1, own, recv_b.at[0])
    (slope_rows,) = rows_inverse(recv_b.at[0], (3,))
    rows_forward(
        [rows_in[1, 0], rows_in[1, 1], rows_in[1, 2] + buo_rows[...] * slope_rows], send_a.at[1]
    )
    own = send_all(2, send_a.at[1], recv_a.at[1])
    for i, t in enumerate(rows_inverse(recv_b.at[0], (0, 1, 2))):
        rows_out[0, i] = t
    rows_out[0, 3] = slope_rows
    own_trac = send_traction(1, 4)
    wait_traction(1, own_trac, 4)
    inner = pl.ds(8, 64)
    for i in range(3):
        t = trac[0, i]
        vpad[i, 1, inner, :] = vpad[i, 1, inner, :] - NEAR * (coef[0, 1] * t)
        vpad[i, 2, inner, :] = vpad[i, 2, inner, :] - FAR * (coef[0, 2] * t)
        k = (XZ, YZ, ZZ)[i]
        spad[k, 0, inner, :] = spad[k, 0, inner, :] + t
    vpad[2, 0, inner, :] = vpad[2, 0, inner, :] + coef[0, 0] * trac[0, 3]
    halo = start_halo(3, vpad, 3, vel_y)
    for copy in halo:
        copy.start()
    outs = [pltpu.make_async_copy(vpad.at[:, :, inner, :], vel_out, out_sem.at[0])]
    outs[-1].start()

    wait_all(2, own, recv_a.at[1])
    spectrum_forward(recv_a.at[1], 1)
    spectrum_inverse(
        [add_lag(i, 0, 1, part[1, i, 0], part[1, i, 1]) for i in range(3)], send_b.at[1]
    )
    own = send_all(3, send_b.at[1], recv_b.at[1])
    outs.append(pltpu.make_async_copy(spec, spe_out, out_sem.at[1]))
    outs[-1].start()

    for copy in halo:
        copy.wait()
    both = edges_of(3)
    for layer in range(4):
        new_stress(both, layer)
    for k in (XX, XY, YY):
        outs.append(
            pltpu.make_async_copy(
                spad.at[k, :, inner, :], str_out.at[PLACE[k]], out_sem.at[2 + k]
            )
        )
        outs[-1].start()
    wait_all(3, own, recv_b.at[1])
    for i, t in enumerate(rows_inverse(recv_b.at[1], (0, 1, 2))):
        rows_out[1, i] = t
    own_trac = send_traction(3, 3)
    wait_traction(3, own_trac, 3)
    for i, k in enumerate((XZ, YZ, ZZ)):
        spad[k, 0, inner, :] = spad[k, 0, inner, :] + trac[1, i]
        outs.append(
            pltpu.make_async_copy(
                spad.at[k, :, inner, :], str_out.at[PLACE[k]], out_sem.at[2 + k]
            )
        )
        outs[-1].start()
    for copy in outs:
        copy.wait()


def on_device(velocity, stress, buoyancy, lame, shear, kernel, history):
    left, right, first, last, small, along = (jnp.asarray(t) for t in tables())
    anyspace = pl.BlockSpec(memory_space=pl.ANY)
    vm, dma = pltpu.VMEM, pltpu.SemaphoreType.DMA
    return pl.pallas_call(
        kernel_body,
        out_shape=(
            jax.ShapeDtypeStruct(velocity.shape, F32),
            jax.ShapeDtypeStruct(stress.shape, F32),
            jax.ShapeDtypeStruct((2, 3, 2, 16, 512), F32),
        ),
        in_specs=[anyspace] * 13,
        out_specs=[anyspace] * 3,
        scratch_shapes=[
            vm((3, 4, 80, 128), F32),
            vm((6, 4, 80, 128), F32),
            vm((3, 4, 64, 128), F32),
            vm((12, 3, 2, 16, 512), BF16),
            vm((11, 3, 2, 16, 512), BF16),
            vm((128, 768), BF16),
            vm((384, 256), BF16),
            vm((128, 256), BF16),
            vm((64, 384), BF16),
            vm((48, 128), F32),
            vm((16, 128), F32),
            vm((4, 64, 128), F32),
            vm((4, 64, 128), F32),
            vm((4, 64, 128), F32),
            vm((2, 3, 64, 128), F32),
            vm((64, 128), F32),
            vm((2, 128, 3, 128), F32),
            vm((2, 128, 3, 128), F32),
            vm((2, 128, 4, 128), F32),
            vm((2, 128, 4, 128), F32),
            vm((2, 4, 64, 128), F32),
            vm((2, 4, 64, 128), F32),
            vm((2, 3, 2, 16, 512), F32),
            vm((2, 3, 2, 16, 512), F32),
            dma((18,)),
            dma((8,)),
            dma((4, 4)),
            dma((4, 4)),
            dma((5,)),
            dma((5,)),
            dma((4,)),
            dma((4,)),
            dma((9,)),
        ],
        compiler_params=pltpu.CompilerParams(
            collective_id=0, has_side_effects=True, vmem_limit_bytes=56 << 20
        ),
    )(
        velocity, stress, buoyancy, lame, shear, kernel, history,
        left, right, first, last, small, along,
    )


def solution(mesh):
    spread = P(None, None, None, ("row", "col"), None)
    return jax.shard_map(
        on_device,
        mesh=mesh,
        in_specs=(
            P(None, None, "row", "col"),
            P(None, None, "row", "col"),
            P(None, "row", "col"),
            P(None, "row", "col"),
            P(None, "row", "col"),
            spread,
            spread,
        ),
        out_specs=(P(None, None, "row", "col"), P(None, None, "row", "col"), spread),
        check_vma=False,
    )
```

profile of v0, /device:TPU:1, one launch (start us, length us, event | category | flops | bytes accessed | tf_op | source)
XLA Modules:
  0.0 66.6 jit_solution(15093387832702814665)
XLA Ops:
  0.6 62.4 %shard_map.148 = (f32[3,4,64,128]{3,2,1,0:T(8,128)}, f32[6,4,64,128]{3,2,1,0:T(8,128)}, f32[2,3,2,16,512]{4,3,2,1,0:T(8,128)}) custom-call(f32[3,4,64,128]{3,2,1,0:T(8,128)} %vel_in.1, f32[6,4,64,128]{3,2,1,0:T(8,128)} %str_in.1, f32[4,64,128]{2,1,0:T(8,128)} %buo_in.1, f32[4,64,128]{2,1,0:T(8,128)} %lam_in.1, f32[4,64,128]{2,1,0:T(8,128)} %she_in.1, ...), custom_call_target="tpu_custom_call" | custom-call | tf_op jit(solution)/shard_map/pallas_call | solution.py:495
  63.1 0.0 copy-start
  63.1 0.0 copy-start.1
  63.1 1.9 %copy.19 = f32[3,4,64,128]{3,2,1,0:T(8,128)} copy(f32[3,4,64,128]{3,2,1,0:T(8,128)} %get-tuple-element.6) | data formatting | bytes 786432
  65.0 0.0 copy-done
  65.0 0.9 %copy.20 = f32[6,4,64,128]{3,2,1,0:T(8,128)} copy(f32[6,4,64,128]{3,2,1,0:T(8,128)S(1)} %copy-done) | data formatting | bytes 1572864
  65.8 0.0 copy-done.1
  65.8 0.7 %copy.21 = f32[2,3,2,16,512]{4,3,2,1,0:T(8,128)} copy(f32[2,3,2,16,512]{4,3,2,1,0:T(8,128)S(1)} %copy-done.1) | data formatting | bytes 786432
Async XLA Ops:
  63.1 1.9 %copy-start = (f32[6,4,64,128]{3,2,1,0:T(8,128)S(1)}, f32[6,4,64,128]{3,2,1,0:T(8,128)}, u32[]{:S(2)}) copy-start(f32[6,4,64,128]{3,2,1,0:T(8,128)} %get-tuple-element.7) | copy-start | bytes 2359300
  63.1 2.8 %copy-start.1 = (f32[2,3,2,16,512]{4,3,2,1,0:T(8,128)S(1)}, f32[2,3,2,16,512]{4,3,2,1,0:T(8,128)}, u32[]{:S(2)}) copy-start(f32[2,3,2,16,512]{4,3,2,1,0:T(8,128)} %get-tuple-element.8) | copy-start | bytes 1179652
where the time goes:
time: 66.7 us; the launch traced here: 66.6 us
  Pallas kernels  62.4 us (94%)
  local copies, waits for them, and re-layouts  3.49 us (5%)
    pallas_call x1, Pallas kernels, on_device(): pl.pallas_call(kernel_body, out_shape=(jax.ShapeDtypeStruct(velocity.shap...  62.4 us
    unnamed x7, local copies, waits for them, and re-layouts  3.49 us

commit v1 on v0

--- a/solution.py
+++ b/solution.py
@@ -52,6 +52,17 @@
     return left, right, first, last, small, along
 
 
+def far_first(count):
+    ring = (0, 1, 2, 1)
+
+    def way(k):
+        row, col = k // COLS, k % COLS
+        z = 2 * (col // 8) + row % 2
+        return ring[row // 2] + ring[z] + ring[col // 2 % 4] + 0.1 * (col % 2)
+
+    return sorted(range(1, count), key=way, reverse=True)
+
+
 def halves(x):
     hi = x.astype(BF16)
     return hi, (x - hi.astype(F32)).astype(BF16)
@@ -64,14 +75,22 @@
 def kernel_body(
     vel_in, str_in, buo_in, lam_in, she_in, ker_in, his_in,
     left_in, right_in, first_in, last_in, small_in, along_in,
-    vel_out, str_out, spe_out,
+    vel_out, str_out, spec,
     vpad, spad, coef, ker, his, left, right, first, last, small, along,
-    pack, pack_low, pack_high, rows_in, buo_rows, send_a, recv_a, send_b, recv_b,
-    rows_out, trac, part, spec,
-    in_sem, out_sem, halo_send, halo_recv, col_send, col_recv, all_send, all_recv, own_sem,
+    pack, pack_low, pack_high, rows_in, buo_rows, send_a, recv_a, send_b, recv_b, send_w, recv_w,
+    rows_out, trac, part,
+    in_sem, halo_send, halo_recv, col_send, col_recv, all_send, all_recv, own_sem, ready,
 ):
     r, c = lax.axis_index("row"), lax.axis_index("col")
     me = r * COLS + c
+
+    def greet(semaphore, row, col):
+        pl.semaphore_signal(semaphore, inc=1, device_id=(row, col), device_id_type=MESH)
+        return 0
+
+    barrier = pltpu.get_barrier_semaphore()
+    lax.fori_loop(1, ROWS, lambda k, _: greet(barrier, lax.rem(r + k, ROWS), c), 0)
+    lax.fori_loop(1, COLS, lambda k, _: greet(barrier, r, lax.rem(c + k, COLS)), 0)
 
     loads = []
 
@@ -93,27 +112,16 @@
     ]
     coef_late = [load(lam_in, coef.at[1]), load(she_in, coef.at[2])]
 
-    def device(k):
-        t = lax.rem(me + k, DEVS)
-        return (t // COLS, lax.rem(t, COLS))
-
-    barrier = pltpu.get_barrier_semaphore()
-
-    def greet(k, _):
-        pl.semaphore_signal(barrier, inc=1, device_id=device(k), device_id_type=MESH)
-        return 0
-
-    lax.fori_loop(1, DEVS, greet, 0)
-
     up, down = (lax.rem(r + 1, ROWS), c), (lax.rem(r + ROWS - 1, ROWS), c)
     after, before = (r, lax.rem(c + 1, COLS)), (r, lax.rem(c + COLS - 1, COLS))
 
     lane = lax.broadcasted_iota(jnp.int32, (64, 128), 1)
     edge = jnp.logical_or(lane < 2, lane >= 126)
 
-    def start_halo(n, pad, count, arrays):
+    def start_halo(n, pad, comps, layers):
         packed = jnp.zeros((64, 128), F32)
-        for k, (comp, layer) in enumerate(arrays):
+        for k in range(3 * len(layers)):
+            comp, layer = comps[k // len(layers)], layers[k % len(layers)]
             f = pad[comp, layer, pl.ds(8, 64), :]
             packed += pltpu.roll(jnp.where(edge, f, 0.0), 4 * k + 2, 1)
         pack[n] = packed
@@ -125,14 +133,17 @@
             )
             return copy
 
+        some = pl.ds(layers[0], len(layers))
         copies = [
-            remote(0, pad.at[pl.ds(0, count), :, pl.ds(64, 8), :],
-                   pad.at[pl.ds(0, count), :, pl.ds(0, 8), :], up),
-            remote(1, pad.at[pl.ds(0, count), :, pl.ds(8, 8), :],
-                   pad.at[pl.ds(0, count), :, pl.ds(72, 8), :], down),
+            remote(0, pad.at[pl.ds(0, 3), some, pl.ds(64, 8), :],
+                   pad.at[pl.ds(0, 3), some, pl.ds(0, 8), :], up),
+            remote(1, pad.at[pl.ds(0, 3), some, pl.ds(8, 8), :],
+                   pad.at[pl.ds(0, 3), some, pl.ds(72, 8), :], down),
             remote(2, pack.at[n], pack_low.at[n], after),
             remote(3, pack.at[n], pack_high.at[n], before),
         ]
+        for copy in copies:
+            copy.start()
         return copies
 
     def edges_of(n):
@@ -160,13 +171,13 @@
                 total = term if total is None else total + term
         return total
 
-    stress_y = [(k, l) for k in (XY, YY, YZ) for l in range(4)]
-    vel_y = [(k, l) for k in range(3) for l in range(4)]
-
-    def new_velocity(both, layer):
+    stress_y, vel_y = (XY, YY, YZ), (0, 1, 2)
+    top, deep, deep4 = (0,), (1, 2, 3), (0, 1, 2, 3)
+
+    def new_velocity(both, layers, layer):
         along_x = [dx(spad, k, layer) for k in (XX, XY, XZ)]
         along_y = [
-            dy(spad[k, layer, pl.ds(8, 64), :], both, 4 * i + layer)
+            dy(spad[k, layer, pl.ds(8, 64), :], both, len(layers) * i + layer - layers[0])
             for i, k in enumerate((XY, YY, YZ))
         ]
         along_z = [dz(spad, k, layer) for k in (XZ, YZ, ZZ)]
@@ -176,7 +187,7 @@
                 along_x[i] + along_y[i] + along_z[i]
             )
 
-    def new_stress(both, layer):
+    def new_stress(both, layer, out=None):
         gx = [dx(vpad, i, layer) for i in range(3)]
         gy = [dy(vpad[i, layer, pl.ds(8, 64), :], both, 4 * i + layer) for i in range(3)]
         gz = [dz(vpad, i, layer) for i in range(3)]
@@ -188,18 +199,19 @@
             XZ: she * (gz[0] + gx[2]), YZ: she * (gz[1] + gy[2]),
         }
         for k, a in adds.items():
-            spad[k, layer, pl.ds(8, 64), :] = spad[k, layer, pl.ds(8, 64), :] + a
+            total = spad[k, layer, pl.ds(8, 64), :] + a
+            if out is None:
+                spad[k, layer, pl.ds(8, 64), :] = total
+            else:
+                out[PLACE[k], layer] = total
 
     def send_rows(n, src, dst):
-        def one(k, _):
-            t = lax.rem(c + k, COLS)
+        for k in far_first(COLS):
+            t = c ^ k
             pltpu.make_async_remote_copy(
                 src_ref=src(t), dst_ref=dst(c), send_sem=col_send.at[n],
                 recv_sem=col_recv.at[n], device_id=(r, t), device_id_type=MESH,
             ).start()
-            return 0
-
-        lax.fori_loop(1, COLS, one, 0)
         own = pltpu.make_async_copy(src(c), dst(c), own_sem.at[n])
         own.start()
         return own
@@ -234,15 +246,12 @@
         wait_rows(n, own, trac.at[n // 2, pl.ds(0, count), pl.ds(0, 60), :])
 
     def send_all(n, src, dst):
-        def one(k, _):
-            t = lax.rem(me + k, DEVS)
+        for k in far_first(DEVS):
             pltpu.make_async_remote_copy(
-                src_ref=src.at[t], dst_ref=dst.at[me], send_sem=all_send.at[n],
-                recv_sem=all_recv.at[n], device_id=device(k), device_id_type=MESH,
+                src_ref=src.at[me ^ k], dst_ref=dst.at[me], send_sem=all_send.at[n],
+                recv_sem=all_recv.at[n], device_id=(r ^ (k // COLS), c ^ (k % COLS)),
+                device_id_type=MESH,
             ).start()
-            return 0
-
-        lax.fori_loop(1, DEVS, one, 0)
         own = pltpu.make_async_copy(src.at[me], dst.at[me], own_sem.at[5 + n])
         own.start()
         return own
@@ -352,45 +361,43 @@
         sr, si = spec[step, i, 0], spec[step, i, 1]
         return re + (kr * sr - ki * si), im + (kr * si + ki * sr)
 
-    for copy in stress_loads:
-        copy.wait()
-    halo = start_halo(0, spad, 3, stress_y)
-    pl.semaphore_wait(barrier, DEVS - 1)
-    for copy in halo:
-        copy.start()
-    for copy in coef_loads:
-        copy.wait()
+    def finish(copies):
+        for copy in copies:
+            copy.wait()
+
+    finish(stress_loads)
+    pl.semaphore_wait(barrier, ROWS + COLS - 2)
+    halo_top = start_halo(0, spad, stress_y, top)
+    lax.fori_loop(1, COLS, lambda k, _: greet(ready, r, lax.rem(c + k, COLS)), 0)
+    halo_deep = start_halo(1, spad, stress_y, deep)
+    finish(coef_loads)
     own_b = send_rows(4, lambda t: coef.at[0, 0, four(t), :], lambda t: buo_rows.at[four(t), :])
-    for copy in conv_loads:
-        copy.wait()
+    finish(conv_loads)
     convolve_past(0)
     vel_load.wait()
-    for copy in halo:
-        copy.wait()
-    both = edges_of(0)
-    new_velocity(both, 0)
+    finish(halo_top)
+    new_velocity(edges_of(0), top, 0)
     own = send_top(0)
-    for layer in range(1, 4):
-        new_velocity(both, layer)
-    halo = start_halo(1, vpad, 3, vel_y)
-    for copy in halo:
-        copy.start()
-    for copy in table_loads:
-        copy.wait()
+    finish(halo_deep)
+    both = edges_of(1)
+    for layer in deep:
+        new_velocity(both, deep, layer)
+    halo = start_halo(2, vpad, vel_y, deep4)
+    convolve_past(1)
+    finish(table_loads)
     wait_top(0, own)
     rows_forward([rows_in[0, i] for i in range(3)], send_a.at[0])
+    pl.semaphore_wait(ready, COLS - 1)
     own = send_all(0, send_a.at[0], recv_a.at[0])
 
-    for copy in coef_late:
-        copy.wait()
-    for copy in halo:
-        copy.wait()
-    both = edges_of(1)
-    for layer in range(4):
+    finish(coef_late)
+    finish(halo)
+    both = edges_of(2)
+    new_stress(both, 0)
+    halo_top = start_halo(3, spad, stress_y, top)
+    for layer in deep:
         new_stress(both, layer)
-    halo = start_halo(2, spad, 3, stress_y)
-    for copy in halo:
-        copy.start()
+    halo_deep = start_halo(4, spad, stress_y, deep)
 
     wait_all(0, own, recv_a.at[0])
     spectrum_forward(recv_a.at[0], 0)
@@ -408,33 +415,44 @@
         )
 
     slopes = (-slope(now[0][1], now[1][1]), slope(now[0][0], now[1][0]))
-    spectrum_inverse([*now, slopes], send_b.at[0])
-    own = send_all(1, send_b.at[0], recv_b.at[0])
-
-    for copy in halo:
-        copy.wait()
-    both = edges_of(2)
-    new_velocity(both, 0)
+    spectrum_inverse([slopes], send_w)
+
+    finish(halo_top)
+    new_velocity(edges_of(3), top, 0)
     own_top = send_top(2)
-    for layer in range(1, 4):
-        new_velocity(both, layer)
-    convolve_past(1)
-    for i in range(3):
-        re, im = add_lag(i, 1, 0, part[1, i, 0], part[1, i, 1])
-        part[1, i, 0], part[1, i, 1] = re, im
+    own = send_all(1, send_w, recv_w)
+    spectrum_inverse(now, send_b.at[0])
+    own_t = send_all(4, send_b.at[0], recv_b.at[0])
     wait_rows(4, own_b, buo_rows.at[pl.ds(0, 60), :])
     wait_top(2, own_top)
 
-    wait_all(1, own, recv_b.at[0])
-    (slope_rows,) = rows_inverse(recv_b.at[0], (3,))
+    wait_all(1, own, recv_w)
+    (slope_rows,) = rows_inverse(recv_w, (0,))
     rows_forward(
         [rows_in[1, 0], rows_in[1, 1], rows_in[1, 2] + buo_rows[...] * slope_rows], send_a.at[1]
     )
     own = send_all(2, send_a.at[1], recv_a.at[1])
+
+    wait_all(4, own_t, recv_b.at[0])
     for i, t in enumerate(rows_inverse(recv_b.at[0], (0, 1, 2))):
         rows_out[0, i] = t
     rows_out[0, 3] = slope_rows
     own_trac = send_traction(1, 4)
+    finish(halo_deep)
+    both = edges_of(4)
+    for layer in deep:
+        new_velocity(both, deep, layer)
+    for i in range(3):
+        re, im = add_lag(i, 1, 0, part[1, i, 0], part[1, i, 1])
+        part[1, i, 0], part[1, i, 1] = re, im
+
+    wait_all(2, own, recv_a.at[1])
+    spectrum_forward(recv_a.at[1], 1)
+    spectrum_inverse(
+        [add_lag(i, 0, 1, part[1, i, 0], part[1, i, 1]) for i in range(3)], send_b.at[1]
+    )
+    own = send_all(3, send_b.at[1], recv_b.at[1])
+
     wait_traction(1, own_trac, 4)
     inner = pl.ds(8, 64)
     for i in range(3):
@@ -444,47 +462,32 @@
         k = (XZ, YZ, ZZ)[i]
         spad[k, 0, inner, :] = spad[k, 0, inner, :] + t
     vpad[2, 0, inner, :] = vpad[2, 0, inner, :] + coef[0, 0] * trac[0, 3]
-    halo = start_halo(3, vpad, 3, vel_y)
-    for copy in halo:
-        copy.start()
-    outs = [pltpu.make_async_copy(vpad.at[:, :, inner, :], vel_out, out_sem.at[0])]
-    outs[-1].start()
-
-    wait_all(2, own, recv_a.at[1])
-    spectrum_forward(recv_a.at[1], 1)
-    spectrum_inverse(
-        [add_lag(i, 0, 1, part[1, i, 0], part[1, i, 1]) for i in range(3)], send_b.at[1]
-    )
-    own = send_all(3, send_b.at[1], recv_b.at[1])
-    outs.append(pltpu.make_async_copy(spec, spe_out, out_sem.at[1]))
-    outs[-1].start()
-
-    for copy in halo:
-        copy.wait()
-    both = edges_of(3)
-    for layer in range(4):
-        new_stress(both, layer)
-    for k in (XX, XY, YY):
-        outs.append(
-            pltpu.make_async_copy(
-                spad.at[k, :, inner, :], str_out.at[PLACE[k]], out_sem.at[2 + k]
-            )
-        )
-        outs[-1].start()
+    halo = start_halo(5, vpad, vel_y, deep4)
+    for i in range(3):
+        for layer in range(4):
+            vel_out[i, layer] = vpad[i, layer, inner, :]
+
     wait_all(3, own, recv_b.at[1])
     for i, t in enumerate(rows_inverse(recv_b.at[1], (0, 1, 2))):
         rows_out[1, i] = t
     own_trac = send_traction(3, 3)
+    finish(halo)
+    both = edges_of(5)
+    for layer in range(4):
+        new_stress(both, layer, str_out)
     wait_traction(3, own_trac, 3)
     for i, k in enumerate((XZ, YZ, ZZ)):
-        spad[k, 0, inner, :] = spad[k, 0, inner, :] + trac[1, i]
-        outs.append(
-            pltpu.make_async_copy(
-                spad.at[k, :, inner, :], str_out.at[PLACE[k]], out_sem.at[2 + k]
-            )
-        )
-        outs[-1].start()
-    for copy in outs:
+        str_out[PLACE[k], 0] = str_out[PLACE[k], 0] + trac[1, i]
+
+
+def store_body(*refs):
+    half = len(refs) // 2
+    copies = [
+        pltpu.make_async_copy(refs[i], refs[half + i], refs[-1].at[i]) for i in range(half)
+    ]
+    for copy in copies:
+        copy.start()
+    for copy in copies:
         copy.wait()
 
 
@@ -492,15 +495,16 @@
     left, right, first, last, small, along = (jnp.asarray(t) for t in tables())
     anyspace = pl.BlockSpec(memory_space=pl.ANY)
     vm, dma = pltpu.VMEM, pltpu.SemaphoreType.DMA
-    return pl.pallas_call(
+    shapes = (
+        jax.ShapeDtypeStruct(velocity.shape, F32),
+        jax.ShapeDtypeStruct(stress.shape, F32),
+        jax.ShapeDtypeStruct((2, 3, 2, 16, 512), F32),
+    )
+    results = pl.pallas_call(
         kernel_body,
-        out_shape=(
-            jax.ShapeDtypeStruct(velocity.shape, F32),
-            jax.ShapeDtypeStruct(stress.shape, F32),
-            jax.ShapeDtypeStruct((2, 3, 2, 16, 512), F32),
-        ),
+        out_shape=tuple(vm(s.shape, s.dtype) for s in shapes),
         in_specs=[anyspace] * 13,
-        out_specs=[anyspace] * 3,
+        out_specs=[pl.BlockSpec(memory_space=pltpu.VMEM)] * 3,
         scratch_shapes=[
             vm((3, 4, 80, 128), F32),
             vm((6, 4, 80, 128), F32),
@@ -513,28 +517,29 @@
             vm((64, 384), BF16),
             vm((48, 128), F32),
             vm((16, 128), F32),
-            vm((4, 64, 128), F32),
-            vm((4, 64, 128), F32),
-            vm((4, 64, 128), F32),
+            vm((6, 64, 128), F32),
+            vm((6, 64, 128), F32),
+            vm((6, 64, 128), F32),
             vm((2, 3, 64, 128), F32),
             vm((64, 128), F32),
             vm((2, 128, 3, 128), F32),
             vm((2, 128, 3, 128), F32),
-            vm((2, 128, 4, 128), F32),
-            vm((2, 128, 4, 128), F32),
+            vm((2, 128, 3, 128), F32),
+            vm((2, 128, 3, 128), F32),
+            vm((128, 1, 128), F32),
+            vm((128, 1, 128), F32),
             vm((2, 4, 64, 128), F32),
             vm((2, 4, 64, 128), F32),
             vm((2, 3, 2, 16, 512), F32),
-            vm((2, 3, 2, 16, 512), F32),
             dma((18,)),
-            dma((8,)),
-            dma((4, 4)),
-            dma((4, 4)),
+            dma((6, 4)),
+            dma((6, 4)),
             dma((5,)),
             dma((5,)),
-            dma((4,)),
-            dma((4,)),
-            dma((9,)),
+            dma((5,)),
+            dma((5,)),
+            dma((10,)),
+            pltpu.SemaphoreType.REGULAR,
         ],
         compiler_params=pltpu.CompilerParams(
             collective_id=0, has_side_effects=True, vmem_limit_bytes=56 << 20
@@ -543,6 +548,14 @@
         velocity, stress, buoyancy, lame, shear, kernel, history,
         left, right, first, last, small, along,
     )
+    return pl.pallas_call(
+        store_body,
+        out_shape=shapes,
+        in_specs=[anyspace] * 3,
+        out_specs=[anyspace] * 3,
+        scratch_shapes=[dma((3,))],
+        compiler_params=pltpu.CompilerParams(vmem_limit_bytes=1 << 20),
+    )(*results)
 
 
 def solution(mesh):

time: 66.7 us -> 56.4 us (0.85)
  Pallas kernels: 62.4 us -> 55.7 us
  local copies, waits for them, and re-layouts: 3.49 us -> 0 us
    pallas_call x1 -> x2, Pallas kernels: 62.4 us -> 55.7 us  [the longest x1 54.5 us: on_device(): pl.pallas_call(kernel_body, out_shape=tuple((vm(s.shape, s.dtype) for s i...]
    unnamed x7 -> x0, local copies, waits for them, and re-layouts: 3.49 us -> none
where the time goes in v1:
time: 56.4 us; the launch traced here: 56.3 us
  Pallas kernels  55.7 us (99%)
  between operations  0.64 us (1%)
    pallas_call x1, Pallas kernels, on_device(): pl.pallas_call(kernel_body, out_shape=tuple((vm(s.shape, s.dtype) for s i...  54.5 us
    pallas_call x1, Pallas kernels, on_device(): pl.pallas_call(store_body, out_shape=shapes, in_specs=[anyspace] * 3, out...  1.16 us

profile of v1, /device:TPU:1, one launch (start us, length us, event | category | flops | bytes accessed | tf_op | source)
XLA Modules:
  0.0 56.3 jit_solution(356893158957142780)
XLA Ops:
  0.6 54.5 %shard_map.148 = (f32[3,4,64,128]{3,2,1,0:T(8,128)S(1)}, f32[6,4,64,128]{3,2,1,0:T(8,128)S(1)}, f32[2,3,2,16,512]{4,3,2,1,0:T(8,128)S(1)}) custom-call(f32[3,4,64,128]{3,2,1,0:T(8,128)} %vel_in.1, f32[6,4,64,128]{3,2,1,0:T(8,128)} %str_in.1, f32[4,64,128]{2,1,0:T(8,128)} %buo_in.1, f32[4,64,128]{2,1,0:T(8,128)} %lam_in.1, f32[4,64,128]{2,1,0:T(8,128)} %she_in.1, ...), custom_call_target="tpu_custom_call" | custom-call | tf_op jit(solution)/shard_map/pallas_call | solution.py:503
  55.2 1.2 %shard_map.149 = (f32[3,4,64,128]{3,2,1,0:T(8,128)}, f32[6,4,64,128]{3,2,1,0:T(8,128)}, f32[2,3,2,16,512]{4,3,2,1,0:T(8,128)}) custom-call(f32[3,4,64,128]{3,2,1,0:T(8,128)S(1)} %get-tuple-element.6.refs_0_, f32[6,4,64,128]{3,2,1,0:T(8,128)S(1)} %get-tuple-element.7.refs_1_, f32[2,3,2,16,512]{4,3,2,1,0:T(8,128)S(1)} %get-tuple-element.8.refs_2_), custom_call_target="tpu_custom_call" | custom-call | tf_op jit(solution)/shard_map/pallas_call | solution.py:551

commit v2 on v1

--- a/solution.py
+++ b/solution.py
@@ -79,19 +79,24 @@
     vpad, spad, coef, ker, his, left, right, first, last, small, along,
     pack, pack_low, pack_high, rows_in, buo_rows, send_a, recv_a, send_b, recv_b, send_w, recv_w,
     rows_out, trac, part,
-    in_sem, halo_send, halo_recv, col_send, col_recv, all_send, all_recv, own_sem, ready,
+    in_sem, halo_send, halo_recv, col_send, col_recv, all_send, all_recv, own_sem, ready_z, ready_y,
 ):
     r, c = lax.axis_index("row"), lax.axis_index("col")
     me = r * COLS + c
 
     def greet(semaphore, row, col):
         pl.semaphore_signal(semaphore, inc=1, device_id=(row, col), device_id_type=MESH)
-        return 0
+
+    up, down = (lax.rem(r + 1, ROWS), c), (lax.rem(r + ROWS - 1, ROWS), c)
+    after, before = (r, lax.rem(c + 1, COLS)), (r, lax.rem(c + COLS - 1, COLS))
+    along_z = [(r, c ^ 8), (r ^ 1, c), (r ^ 1, c ^ 8)]
+    along_y = [(r ^ 4, c), (r ^ 2, c), (r ^ 6, c)]
+    along_x = [(r, c ^ k) for k in (5, 4, 7, 6, 3, 2, 1)]
+    near = [after, before, up, down, *along_y, *along_z, *along_x]
 
     barrier = pltpu.get_barrier_semaphore()
-    lax.fori_loop(1, ROWS, lambda k, _: greet(barrier, lax.rem(r + k, ROWS), c), 0)
-    lax.fori_loop(1, COLS, lambda k, _: greet(barrier, r, lax.rem(c + k, COLS)), 0)
-
+    for mate in near:
+        greet(barrier, *mate)
     loads = []
 
     def load(src, dst):
@@ -112,13 +117,10 @@
     ]
     coef_late = [load(lam_in, coef.at[1]), load(she_in, coef.at[2])]
 
-    up, down = (lax.rem(r + 1, ROWS), c), (lax.rem(r + ROWS - 1, ROWS), c)
-    after, before = (r, lax.rem(c + 1, COLS)), (r, lax.rem(c + COLS - 1, COLS))
-
     lane = lax.broadcasted_iota(jnp.int32, (64, 128), 1)
     edge = jnp.logical_or(lane < 2, lane >= 126)
 
-    def start_halo(n, pad, comps, layers):
+    def make_halo(n, pad, comps, layers):
         packed = jnp.zeros((64, 128), F32)
         for k in range(3 * len(layers)):
             comp, layer = comps[k // len(layers)], layers[k % len(layers)]
@@ -142,8 +144,15 @@
             remote(2, pack.at[n], pack_low.at[n], after),
             remote(3, pack.at[n], pack_high.at[n], before),
         ]
+        return copies
+
+    def begin(copies):
         for copy in copies:
             copy.start()
+
+    def start_halo(n, pad, comps, layers):
+        copies = make_halo(n, pad, comps, layers)
+        begin(copies)
         return copies
 
     def edges_of(n):
@@ -245,13 +254,17 @@
     def wait_traction(n, own, count):
         wait_rows(n, own, trac.at[n // 2, pl.ds(0, count), pl.ds(0, 60), :])
 
-    def send_all(n, src, dst):
-        for k in far_first(DEVS):
+    order = far_first(DEVS)
+
+    def send_all(n, src, dst, some=order):
+        for k in some:
             pltpu.make_async_remote_copy(
                 src_ref=src.at[me ^ k], dst_ref=dst.at[me], send_sem=all_send.at[n],
                 recv_sem=all_recv.at[n], device_id=(r ^ (k // COLS), c ^ (k % COLS)),
                 device_id_type=MESH,
             ).start()
+        if some[-1] != order[-1]:
+            return None
         own = pltpu.make_async_copy(src.at[me], dst.at[me], own_sem.at[5 + n])
         own.start()
         return own
@@ -366,28 +379,34 @@
             copy.wait()
 
     finish(stress_loads)
-    pl.semaphore_wait(barrier, ROWS + COLS - 2)
-    halo_top = start_halo(0, spad, stress_y, top)
-    lax.fori_loop(1, COLS, lambda k, _: greet(ready, r, lax.rem(c + k, COLS)), 0)
-    halo_deep = start_halo(1, spad, stress_y, deep)
-    finish(coef_loads)
-    own_b = send_rows(4, lambda t: coef.at[0, 0, four(t), :], lambda t: buo_rows.at[four(t), :])
+    halo_top = make_halo(0, spad, stress_y, top)
+    halo_deep = make_halo(1, spad, stress_y, deep)
     finish(conv_loads)
     convolve_past(0)
+    pl.semaphore_wait(barrier, len(near))
+    begin(halo_top)
+    for mate in along_z:
+        greet(ready_z, *mate)
+    begin(halo_deep)
+    convolve_past(1)
+    finish(coef_loads)
     vel_load.wait()
     finish(halo_top)
     new_velocity(edges_of(0), top, 0)
+    pl.semaphore_wait(ready_z, len(along_z))
     own = send_top(0)
+    for mate in along_y:
+        greet(ready_y, *mate)
+    own_b = send_rows(4, lambda t: coef.at[0, 0, four(t), :], lambda t: buo_rows.at[four(t), :])
     finish(halo_deep)
     both = edges_of(1)
     for layer in deep:
         new_velocity(both, deep, layer)
     halo = start_halo(2, vpad, vel_y, deep4)
-    convolve_past(1)
     finish(table_loads)
     wait_top(0, own)
     rows_forward([rows_in[0, i] for i in range(3)], send_a.at[0])
-    pl.semaphore_wait(ready, COLS - 1)
+    pl.semaphore_wait(ready_y, len(along_y))
     own = send_all(0, send_a.at[0], recv_a.at[0])
 
     finish(coef_late)
@@ -417,10 +436,11 @@
     slopes = (-slope(now[0][1], now[1][1]), slope(now[0][0], now[1][0]))
     spectrum_inverse([slopes], send_w)
 
+    send_all(1, send_w, recv_w, order[:80])
     finish(halo_top)
     new_velocity(edges_of(3), top, 0)
     own_top = send_top(2)
-    own = send_all(1, send_w, recv_w)
+    own = send_all(1, send_w, recv_w, order[80:])
     spectrum_inverse(now, send_b.at[0])
     own_t = send_all(4, send_b.at[0], recv_b.at[0])
     wait_rows(4, own_b, buo_rows.at[pl.ds(0, 60), :])
@@ -540,6 +560,7 @@
             dma((5,)),
             dma((10,)),
             pltpu.SemaphoreType.REGULAR,
+            pltpu.SemaphoreType.REGULAR,
         ],
         compiler_params=pltpu.CompilerParams(
             collective_id=0, has_side_effects=True, vmem_limit_bytes=56 << 20

time: 56.4 us -> 55.6 us (0.986)
  Pallas kernels: 55.7 us -> 54.8 us
    pallas_call x1, Pallas kernels: 54.5 us -> 53.6 us  [on_device(): pl.pallas_call(kernel_body, out_shape=tuple((vm(s.shape, s.dtype) for s i...]
where the time goes in v2:
time: 55.6 us; the launch traced here: 55.4 us
  Pallas kernels  54.8 us (99%)
  between operations  0.64 us (1%)
    pallas_call x1, Pallas kernels, on_device(): pl.pallas_call(kernel_body, out_shape=tuple((vm(s.shape, s.dtype) for s i...  53.6 us
    pallas_call x1, Pallas kernels, on_device(): pl.pallas_call(store_body, out_shape=shapes, in_specs=[anyspace] * 3, out...  1.16 us

profile of v2, /device:TPU:1, one launch (start us, length us, event | category | flops | bytes accessed | tf_op | source)
XLA Modules:
  0.0 55.4 jit_solution(4297180580259233228)
XLA Ops:
  0.6 53.6 %shard_map.148 = (f32[3,4,64,128]{3,2,1,0:T(8,128)S(1)}, f32[6,4,64,128]{3,2,1,0:T(8,128)S(1)}, f32[2,3,2,16,512]{4,3,2,1,0:T(8,128)S(1)}) custom-call(f32[3,4,64,128]{3,2,1,0:T(8,128)} %vel_in.1, f32[6,4,64,128]{3,2,1,0:T(8,128)} %str_in.1, f32[4,64,128]{2,1,0:T(8,128)} %buo_in.1, f32[4,64,128]{2,1,0:T(8,128)} %lam_in.1, f32[4,64,128]{2,1,0:T(8,128)} %she_in.1, ...), custom_call_target="tpu_custom_call" | custom-call | tf_op jit(solution)/shard_map/pallas_call | solution.py:523
  54.3 1.2 %shard_map.149 = (f32[3,4,64,128]{3,2,1,0:T(8,128)}, f32[6,4,64,128]{3,2,1,0:T(8,128)}, f32[2,3,2,16,512]{4,3,2,1,0:T(8,128)}) custom-call(f32[3,4,64,128]{3,2,1,0:T(8,128)S(1)} %get-tuple-element.6.refs_0_, f32[6,4,64,128]{3,2,1,0:T(8,128)S(1)} %get-tuple-element.7.refs_1_, f32[2,3,2,16,512]{4,3,2,1,0:T(8,128)S(1)} %get-tuple-element.8.refs_2_), custom_call_target="tpu_custom_call" | custom-call | tf_op jit(solution)/shard_map/pallas_call | solution.py:572

commit v3 on v2

--- a/solution.py
+++ b/solution.py
@@ -281,7 +281,7 @@
     def turn(re, im, cos, sin, sign):
         return re * cos - im * (sign * sin), im * cos + re * (sign * sin)
 
-    def to_send(blocks, sign, out):
+    def to_send(blocks, sign, out, place=0):
         data = []
         for re, im in blocks:
             data.append(jnp.concatenate([re, -sign * im], axis=1))
@@ -289,7 +289,7 @@
         hi, lo = halves(jnp.concatenate(data, axis=0))
         full = dot(left[...], jnp.concatenate([hi, lo, hi], axis=1), ((1,), (1,)))
         for i in range(len(blocks)):
-            out[:, i, :] = full[:, 128 * i : 128 * i + 128]
+            out[:, place + i, :] = full[:, 128 * i : 128 * i + 128]
 
     def from_recv(buf, which, sign):
         turned = [buf[:, i, :].T for i in which]
@@ -302,7 +302,7 @@
             result.append((p[:64] - sign * q[64:], p[64:] + sign * q[:64]))
         return result
 
-    def rows_forward(fields, out):
+    def rows_forward(fields, out, place=0):
         hi, lo = halves(jnp.concatenate(fields, axis=1))
         mixed = dot(first[...], jnp.concatenate([hi, lo, hi, lo], axis=0))
         cos, sin = small[0:16][None], small[16:32][None]
@@ -312,7 +312,7 @@
             re, im = a[:64].reshape(4, 16, 128), a[64:].reshape(4, 16, 128)
             re, im = turn(re, im, cos, sin, -1.0)
             blocks.append((re.reshape(64, 128), im.reshape(64, 128)))
-        to_send(blocks, -1.0, out)
+        to_send(blocks, -1.0, out, place)
 
     def rows_inverse(buf, which):
         cos, sin = small[0:16][None], small[16:32][None]
@@ -397,7 +397,6 @@
     own = send_top(0)
     for mate in along_y:
         greet(ready_y, *mate)
-    own_b = send_rows(4, lambda t: coef.at[0, 0, four(t), :], lambda t: buo_rows.at[four(t), :])
     finish(halo_deep)
     both = edges_of(1)
     for layer in deep:
@@ -408,6 +407,7 @@
     rows_forward([rows_in[0, i] for i in range(3)], send_a.at[0])
     pl.semaphore_wait(ready_y, len(along_y))
     own = send_all(0, send_a.at[0], recv_a.at[0])
+    own_b = send_rows(4, lambda t: coef.at[0, 0, four(t), :], lambda t: buo_rows.at[four(t), :])
 
     finish(coef_late)
     finish(halo)
@@ -445,12 +445,11 @@
     own_t = send_all(4, send_b.at[0], recv_b.at[0])
     wait_rows(4, own_b, buo_rows.at[pl.ds(0, 60), :])
     wait_top(2, own_top)
+    rows_forward([rows_in[1, 0], rows_in[1, 1]], send_a.at[1])
 
     wait_all(1, own, recv_w)
     (slope_rows,) = rows_inverse(recv_w, (0,))
-    rows_forward(
-        [rows_in[1, 0], rows_in[1, 1], rows_in[1, 2] + buo_rows[...] * slope_rows], send_a.at[1]
-    )
+    rows_forward([rows_in[1, 2] + buo_rows[...] * slope_rows], send_a.at[1], 2)
     own = send_all(2, send_a.at[1], recv_a.at[1])
 
     wait_all(4, own_t, recv_b.at[0])

time: 55.6 us -> 55.4 us (level)
  no operation moved by 1% of the time
where the time goes in v3:
time: 55.4 us; the launch traced here: 55.3 us
  Pallas kernels  54.7 us (99%)
  between operations  0.64 us (1%)
    pallas_call x1, Pallas kernels, on_device(): pl.pallas_call(kernel_body, out_shape=tuple((vm(s.shape, s.dtype) for s i...  53.5 us
    pallas_call x1, Pallas kernels, on_device(): pl.pallas_call(store_body, out_shape=shapes, in_specs=[anyspace] * 3, out...  1.16 us

profile of v3, /device:TPU:1, one launch (start us, length us, event | category | flops | bytes accessed | tf_op | source)
XLA Modules:
  0.0 55.3 jit_solution(6379245931688854838)
XLA Ops:
  0.6 53.5 %shard_map.148 = (f32[3,4,64,128]{3,2,1,0:T(8,128)S(1)}, f32[6,4,64,128]{3,2,1,0:T(8,128)S(1)}, f32[2,3,2,16,512]{4,3,2,1,0:T(8,128)S(1)}) custom-call(f32[3,4,64,128]{3,2,1,0:T(8,128)} %vel_in.1, f32[6,4,64,128]{3,2,1,0:T(8,128)} %str_in.1, f32[4,64,128]{2,1,0:T(8,128)} %buo_in.1, f32[4,64,128]{2,1,0:T(8,128)} %lam_in.1, f32[4,64,128]{2,1,0:T(8,128)} %she_in.1, ...), custom_call_target="tpu_custom_call" | custom-call | tf_op jit(solution)/shard_map/pallas_call | solution.py:522
  54.2 1.2 %shard_map.149 = (f32[3,4,64,128]{3,2,1,0:T(8,128)}, f32[6,4,64,128]{3,2,1,0:T(8,128)}, f32[2,3,2,16,512]{4,3,2,1,0:T(8,128)}) custom-call(f32[3,4,64,128]{3,2,1,0:T(8,128)S(1)} %get-tuple-element.6.refs_0_, f32[6,4,64,128]{3,2,1,0:T(8,128)S(1)} %get-tuple-element.7.refs_1_, f32[2,3,2,16,512]{4,3,2,1,0:T(8,128)S(1)} %get-tuple-element.8.refs_2_), custom_call_target="tpu_custom_call" | custom-call | tf_op jit(solution)/shard_map/pallas_call | solution.py:571
